TPU v7x, 32 devices: a whole 2x2x4 slice. The times are simulated.
32 devices in a mesh: seq: 8 (over z, y), txt: 4 (over x, core).
Axes of the slice: x: 2, y: 2, z: 4, core: 2. Of those that a mesh axis runs over, the one named last changes fastest.
Arguments:
- self_q: bfloat16 [3072, 1024], P('seq', 'txt'), may hold values from -8 to 8
- self_k: bfloat16 [3072, 1024], P('seq', 'txt'), may hold values from -8 to 8
- self_v: bfloat16 [3072, 1024], P('seq', 'txt'), may hold values from -6 to 6
- cross_q: bfloat16 [3072, 1024], P('seq', 'txt'), may hold values from -8 to 8
- text_k: bfloat16 [4096, 1024], P('txt'), may hold values from -8 to 8
- text_v: bfloat16 [4096, 1024], P('txt'), may hold values from -6 to 6
- lags: int32 [24], P('seq'), may hold values from 1 to 32, as said below
Outputs:
- self_out: bfloat16 [3072, 1024], P('seq', 'txt')
- cross_out: bfloat16 [3072, 1024], P('seq', 'txt')
Inputs may be any that keep to these rules, and one draw needn't show every extreme that they name: lags never fall from one span to the next; the last span sees all 32 blocks.
All inputs are finite; a program needn't handle non-finite values.
Results may differ from a plain program's by a relative error of at most 0.014.
Values may be sent and summed in bfloat16 or wider, within the bound.
A program may use at most 128 MiB of HBM per device.

v0:
```python
import math

import jax
import jax.numpy as jnp
from jax import lax
from jax.sharding import PartitionSpec as P

HSIZE = 128
SPAN = 128
TBLK = 128


NEG_FILL = -1e30


def scale_columns(weighted, scale):
    rows = weighted.shape[0]
    heads = scale.shape[0]
    shaped = weighted.reshape(rows, heads, weighted.shape[1] // heads)
    return (shaped * jnp.transpose(scale)[:, :, None]).reshape(rows, weighted.shape[1])


def softmax_update(state, query, keys, values, visible, factor):
    running, totals, weighted = state
    heads = running.shape[0]
    peaks = []
    sums = []
    columns = []
    for head in range(heads):
        low = head * HSIZE
        high = low + HSIZE
        scores = (
            lax.dot_general(
                query[:, low:high],
                keys[:, low:high],
                (((1,), (1,)), ((), ())),
                preferred_element_type=jnp.float32,
            )
            * factor
        )
        scores = jnp.where(visible, scores, NEG_FILL)
        peak = jnp.maximum(running[head], jnp.max(scores, axis=1))
        probs = jnp.where(visible, jnp.exp(scores - peak[:, None]), 0.0)
        shrink = jnp.exp(running[head] - peak)
        sums.append(totals[head] * shrink + jnp.sum(probs, axis=1))
        mixed = jnp.dot(
            probs.astype(jnp.bfloat16), values[:, low:high], preferred_element_type=jnp.float32
        )
        columns.append(weighted[:, low:high] * shrink[:, None] + mixed)
        peaks.append(peak)
    return (jnp.stack(peaks), jnp.stack(sums), jnp.concatenate(columns, axis=1))


def empty_state(heads, rows, width):
    return (
        jnp.full((heads, rows), NEG_FILL, jnp.float32),
        jnp.zeros((heads, rows), jnp.float32),
        jnp.zeros((rows, heads * width), jnp.float32),
    )


def finish(state):
    return scale_columns(state[2], 1.0 / state[1]).astype(jnp.bfloat16)


def per_device(self_q, self_k, self_v, cross_q, text_k, text_v, lags):
    rows = self_q.shape[0]
    half = rows // 2
    local_heads = self_q.shape[1] // HSIZE
    factor = 1.0 / math.sqrt(HSIZE)
    place = lax.axis_index("seq")
    offsets = jnp.arange(half, dtype=jnp.int32)
    lower = self_q[:half]
    upper = self_q[half:]
    upper_pos = place * rows + half + offsets
    positions = [place * rows + offsets, upper_pos]
    groups = [lower, upper]

    def visit(states, key_block, value_block, first, length):
        key_pos = first + jnp.arange(length, dtype=jnp.int32)
        updated = []
        for group in range(2):
            visible = key_pos[None, :] <= positions[group][:, None]
            query = groups[group]
            updated.append(
                lax.cond(
                    first <= positions[group][half - 1],
                    lambda state: softmax_update(
                        state, query, key_block, value_block, visible, factor
                    ),
                    lambda state: state,
                    states[group],
                )
            )
        return tuple(updated)

    initial = (empty_state(local_heads, half, HSIZE), empty_state(local_heads, half, HSIZE))
    carry = initial
    keys = lax.all_gather(self_k, "seq", axis=0, tiled=True)
    values = lax.all_gather(self_v, "seq", axis=0, tiled=True)
    length = keys.shape[0]
    block = 512
    width = keys.shape[1]
    key_blocks = keys.reshape(length // block, block, width)
    value_blocks = values.reshape(length // block, block, width)

    def one_block(states, inputs):
        key_block, value_block, number = inputs
        return (visit(states, key_block, value_block, number * block, block), None)

    carry, _ = lax.scan(
        one_block, carry, (key_blocks, value_blocks, jnp.arange(length // block, dtype=jnp.int32))
    )
    states = carry
    lower_out = finish(states[0])
    upper_out = finish(states[1])
    self_out = jnp.concatenate([lower_out, upper_out], axis=0)
    limits = jnp.repeat(lags * TBLK, SPAN)
    whole_keys, whole_values = (
        lax.all_to_all(text_k, "txt", split_axis=1, concat_axis=0, tiled=True),
        lax.all_to_all(text_v, "txt", split_axis=1, concat_axis=0, tiled=True),
    )
    text_rows = whole_keys.shape[0]
    visible = jnp.arange(text_rows, dtype=jnp.int32)[None, :] < limits[:, None]
    cross_state = softmax_update(
        empty_state(local_heads, rows, HSIZE), cross_q, whole_keys, whole_values, visible, factor
    )
    cross_out = finish(cross_state)
    return (self_out, cross_out)


def solution(mesh):
    return jax.shard_map(
        per_device,
        mesh=mesh,
        in_specs=(
            P("seq", "txt"),
            P("seq", "txt"),
            P("seq", "txt"),
            P("seq", "txt"),
            P("txt", None),
            P("txt", None),
            P("seq"),
        ),
        out_specs=(P("seq", "txt"), P("seq", "txt")),
        check_vma=False,
    )
```

profile of v0, /device:TPU:24, one launch (start us, length us, event | category | flops | bytes accessed | tf_op | source)
XLA Modules:
  0.0 155.1 jit_solution(18280298507933847203)
XLA Ops:
  7.9 4.0 %copy.17 = bf16[1024,1024]{0,1:T(8,128)(2,1)} copy(bf16[1024,1024]{1,0:T(8,128)(2,1)} %param.17) | data formatting | bytes 4194304 | tf_op args[4]
  11.9 3.6 %all-to-all-start = ((bf16[1024,4,256]{0,2,1:T(8,128)(2,1)}), bf16[1024,4,256]{0,2,1:T(8,128)(2,1)S(1)}, u32[]{:S(2)}, u32[]{:S(2)}) async-start(bf16[1024,4,256]{0,2,1:T(8,128)(2,1)} %bitcast.56), calls=%async_computation | async-start | bytes 4194304 | tf_op jit(solution)/shard_map/all_to_all | solution.py:120
  16.3 4.0 %copy.19 = bf16[1024,1024]{0,1:T(8,128)(2,1)} copy(bf16[1024,1024]{1,0:T(8,128)(2,1)} %param.18) | data formatting | bytes 4194304 | tf_op args[5]
  20.4 20.8 %all-to-all-done = bf16[1024,4,256]{0,2,1:T(8,128)(2,1)S(1)} async-done(((bf16[1024,4,256]{0,2,1:T(8,128)(2,1)}), bf16[1024,4,256]{0,2,1:T(8,128)(2,1)S(1)}, u32[]{:S(2)}, u32[]{:S(2)}) %all-to-all-start) | async-done | bytes 2097184 | tf_op jit(solution)/shard_map/all_to_all | solution.py:120
  41.2 4.5 %all-to-all-start.1 = ((bf16[1024,4,256]{0,2,1:T(8,128)(2,1)}), bf16[1024,4,256]{0,2,1:T(8,128)(2,1)}, u32[]{:S(2)}, u32[]{:S(2)}) async-start(bf16[1024,4,256]{0,2,1:T(8,128)(2,1)} %bitcast.25), calls=%async_computation.1 | async-start | bytes 4194304 | tf_op jit(solution)/shard_map/all_to_all | solution.py:121
  45.7 2.6 %copy.18 = bf16[4,1024,256]{2,1,0:T(8,128)(2,1)} copy(bf16[4,1024,256]{1,2,0:T(8,128)(2,1)S(1)} %bitcast.55) | data formatting | bytes 4194304 | tf_op jit(solution)/shard_map/all_to_all | solution.py:120
  48.2 2.8 %fusion.83 = (f32[384]{0:T(512)S(1)}, f32[384,4096]{1,0:T(8,128)S(1)}) fusion(bf16[4096,256]{1,0:T(8,128)(2,1)} %bitcast.61, bf16[384,256]{1,0:T(8,128)(2,1)S(1)} %copy-done.5, s32[384]{0:T(512)S(1)} %broadcast_bitcast_fusion), kind=kOutput, calls=%fused_computation.126 | convolution fusion | flops 408944256 | bytes 7441920 | tf_op jit(solution)/shard_map/dot_general | solution.py:33
  51.0 1.4 fusion.84
  52.4 3.3 %fusion.48 = (f32[384]{0:T(512)S(1)}, f32[384]{0:T(512)S(1)}) fusion(f32[384,4096]{1,0:T(8,128)S(1)} %get-tuple-element.240, f32[384]{0:T(512)S(1)} %broadcast_maximum_fusion.1, s32[384]{0:T(512)S(1)} %broadcast_bitcast_fusion, f32[384,4096]{1,0:T(8,128)S(1)} %get-tuple-element.238, f32[384]{0:T(512)S(1)} %broadcast_maximum_fusion), kind=kLoop, calls=%fused_computation.82 | loop fusion | flops 11009280 | bytes 12590592 | tf_op jit(solution)/shard_map/reduce_sum | solution.py:45
  55.8 15.7 %all-to-all-done.1 = bf16[1024,4,256]{0,2,1:T(8,128)(2,1)} async-done(((bf16[1024,4,256]{0,2,1:T(8,128)(2,1)}), bf16[1024,4,256]{0,2,1:T(8,128)(2,1)}, u32[]{:S(2)}, u32[]{:S(2)}) %all-to-all-start.1) | async-done | bytes 2097184 | tf_op jit(solution)/shard_map/all_to_all | solution.py:121
  71.4 4.1 %copy.20 = bf16[4,1024,256]{2,1,0:T(8,128)(2,1)} copy(bf16[4,1024,256]{1,2,0:T(8,128)(2,1)} %bitcast.26) | data formatting | bytes 4194304 | tf_op jit(solution)/shard_map/all_to_all | solution.py:121
  75.5 4.8 %fusion.56 = f32[384,128]{0,1:T(8,128)S(1)} fusion(f32[384,4096]{1,0:T(8,128)} %copy-done.1, f32[384]{0:T(512)S(1)} %broadcast_maximum_fusion.1, s32[384]{0:T(512)S(1)} %broadcast_bitcast_fusion, bf16[4096,256]{1,0:T(8,128)(2,1)} %bitcast.59, f32[384]{0:T(512)S(1)} %get-tuple-element.234), kind=kOutput, calls=%fused_computation.88 | convolution fusion | flops 408993792 | bytes 7541248 | tf_op jit(solution)/shard_map/dot_general | solution.py:46
  80.4 1.6 %fusion.59 = f32[384,128]{0,1:T(8,128)S(1)} fusion(f32[384,4096]{1,0:T(8,128)S(1)} %bitcast.58, f32[384]{0:T(512)S(1)} %broadcast_maximum_fusion, s32[384]{0:T(512)S(1)} %broadcast_bitcast_fusion, bf16[4096,256]{1,0:T(8,128)(2,1)S(1)} %bitcast.60, f32[384]{0:T(512)S(1)} %get-tuple-element.243), kind=kOutput, calls=%fused_computation.89 | convolution fusion | flops 408993792 | bytes 7542784 | tf_op jit(solution)/shard_map/dot_general | solution.py:46
  82.9 16.1 %all-gather.5.cloned.1.call-done = bf16[3072,256]{1,0:T(8,128)(2,1)} async-done(((bf16[384,256]{1,0:T(8,128)(2,1)}), bf16[3072,256]{1,0:T(8,128)(2,1)}) %all-gather.5.cloned.1.call-update) | async-done | bytes 1572880 | tf_op jit(solution)/shard_map/all_gather | solution.py:100
  99.1 47.5 %while.20 = (s32[]{:T(128)}, f32[2,192]{1,0:T(2,128)S(1)}, f32[2,192]{1,0:T(2,128)S(1)}, f32[192,256]{1,0:T(8,128)S(1)}, f32[2,192]{1,0:T(2,128)S(1)}, /*index=5...) while((s32[]{:T(128)}, f32[2,192]{1,0:T(2,128)S(1)}, ...), condition=%wide.region_13.14_spmd, body=%wide.region_0.13_spmd.sunk | while | flops 206148608 | bytes 8684497 | solution.py:111
  100.4 1.1 dynamic-slice_bitcast_fusion.3
  102.8 1.6 %conditional.5 = ((f32[2,192]{1,0:T(2,128)S(1)}, f32[2,192]{1,0:T(2,128)S(1)}, f32[192,256]{1,0:T(8,128)S(1)})) conditional(s32[]{:T(128)} %convert_element_type.60, (f32[2,192]{1,0:T(2,128)S(1)}, f32[2,192]{1,0:T(2,128)S(1)}, f32[192,256]{1,0:T(8,128)S(1)}) %tuple.81, (f32[2,192]{1,0:T(2,128)S(1)}, s32[512]{0:T(512)S(1)}, s32[192]{0:T(256)S(1)}, ...), branch_computations={%region_7.7_spmd, %region_8.12_spmd} | conditional | flops 103074048 | bytes 3816736 | solution.py:86
  105.7 1.6 %conditional.4 = ((f32[2,192]{1,0:T(2,128)S(1)}, f32[2,192]{1,0:T(2,128)S(1)}, f32[192,256]{1,0:T(8,128)S(1)})) conditional(s32[]{:T(128)} %convert_element_type.59, (f32[2,192]{1,0:T(2,128)S(1)}, f32[2,192]{1,0:T(2,128)S(1)}, f32[192,256]{1,0:T(8,128)S(1)}) %tuple.79, (f32[2,192]{1,0:T(2,128)S(1)}, s32[512]{0:T(512)S(1)}, s32[192]{0:T(256)S(1)}, ...), branch_computations={%region_1.1_spmd, %region_2.6_spmd} | conditional | flops 103074048 | bytes 3816736 | solution.py:86
  108.6 1.1 dynamic-slice_bitcast_fusion.3
  111.0 1.6 %conditional.5 = ((f32[2,192]{1,0:T(2,128)S(1)}, f32[2,192]{1,0:T(2,128)S(1)}, f32[192,256]{1,0:T(8,128)S(1)})) conditional(s32[]{:T(128)} %convert_element_type.60, (f32[2,192]{1,0:T(2,128)S(1)}, f32[2,192]{1,0:T(2,128)S(1)}, f32[192,256]{1,0:T(8,128)S(1)}) %tuple.81, (f32[2,192]{1,0:T(2,128)S(1)}, s32[512]{0:T(512)S(1)}, s32[192]{0:T(256)S(1)}, ...), branch_computations={%region_7.7_spmd, %region_8.12_spmd} | conditional | flops 103074048 | bytes 3816736 | solution.py:86
  113.9 1.6 %conditional.4 = ((f32[2,192]{1,0:T(2,128)S(1)}, f32[2,192]{1,0:T(2,128)S(1)}, f32[192,256]{1,0:T(8,128)S(1)})) conditional(s32[]{:T(128)} %convert_element_type.59, (f32[2,192]{1,0:T(2,128)S(1)}, f32[2,192]{1,0:T(2,128)S(1)}, f32[192,256]{1,0:T(8,128)S(1)}) %tuple.79, (f32[2,192]{1,0:T(2,128)S(1)}, s32[512]{0:T(512)S(1)}, s32[192]{0:T(256)S(1)}, ...), branch_computations={%region_1.1_spmd, %region_2.6_spmd} | conditional | flops 103074048 | bytes 3816736 | solution.py:86
  116.8 1.1 dynamic-slice_bitcast_fusion.3
  119.1 1.6 %conditional.5 = ((f32[2,192]{1,0:T(2,128)S(1)}, f32[2,192]{1,0:T(2,128)S(1)}, f32[192,256]{1,0:T(8,128)S(1)})) conditional(s32[]{:T(128)} %convert_element_type.60, (f32[2,192]{1,0:T(2,128)S(1)}, f32[2,192]{1,0:T(2,128)S(1)}, f32[192,256]{1,0:T(8,128)S(1)}) %tuple.81, (f32[2,192]{1,0:T(2,128)S(1)}, s32[512]{0:T(512)S(1)}, s32[192]{0:T(256)S(1)}, ...), branch_computations={%region_7.7_spmd, %region_8.12_spmd} | conditional | flops 103074048 | bytes 3816736 | solution.py:86
  122.1 1.6 %conditional.4 = ((f32[2,192]{1,0:T(2,128)S(1)}, f32[2,192]{1,0:T(2,128)S(1)}, f32[192,256]{1,0:T(8,128)S(1)})) conditional(s32[]{:T(128)} %convert_element_type.59, (f32[2,192]{1,0:T(2,128)S(1)}, f32[2,192]{1,0:T(2,128)S(1)}, f32[192,256]{1,0:T(8,128)S(1)}) %tuple.79, (f32[2,192]{1,0:T(2,128)S(1)}, s32[512]{0:T(512)S(1)}, s32[192]{0:T(256)S(1)}, ...), branch_computations={%region_1.1_spmd, %region_2.6_spmd} | conditional | flops 103074048 | bytes 3816736 | solution.py:86
  125.0 1.1 dynamic-slice_bitcast_fusion.3
  127.3 1.6 %conditional.5 = ((f32[2,192]{1,0:T(2,128)S(1)}, f32[2,192]{1,0:T(2,128)S(1)}, f32[192,256]{1,0:T(8,128)S(1)})) conditional(s32[]{:T(128)} %convert_element_type.60, (f32[2,192]{1,0:T(2,128)S(1)}, f32[2,192]{1,0:T(2,128)S(1)}, f32[192,256]{1,0:T(8,128)S(1)}) %tuple.81, (f32[2,192]{1,0:T(2,128)S(1)}, s32[512]{0:T(512)S(1)}, s32[192]{0:T(256)S(1)}, ...), branch_computations={%region_7.7_spmd, %region_8.12_spmd} | conditional | flops 103074048 | bytes 3816736 | solution.py:86
  130.3 1.6 %conditional.4 = ((f32[2,192]{1,0:T(2,128)S(1)}, f32[2,192]{1,0:T(2,128)S(1)}, f32[192,256]{1,0:T(8,128)S(1)})) conditional(s32[]{:T(128)} %convert_element_type.59, (f32[2,192]{1,0:T(2,128)S(1)}, f32[2,192]{1,0:T(2,128)S(1)}, f32[192,256]{1,0:T(8,128)S(1)}) %tuple.79, (f32[2,192]{1,0:T(2,128)S(1)}, s32[512]{0:T(512)S(1)}, s32[192]{0:T(256)S(1)}, ...), branch_computations={%region_1.1_spmd, %region_2.6_spmd} | conditional | flops 103074048 | bytes 3816736 | solution.py:86
  133.2 1.1 dynamic-slice_bitcast_fusion.3
  135.5 1.6 %conditional.5 = ((f32[2,192]{1,0:T(2,128)S(1)}, f32[2,192]{1,0:T(2,128)S(1)}, f32[192,256]{1,0:T(8,128)S(1)})) conditional(s32[]{:T(128)} %convert_element_type.60, (f32[2,192]{1,0:T(2,128)S(1)}, f32[2,192]{1,0:T(2,128)S(1)}, f32[192,256]{1,0:T(8,128)S(1)}) %tuple.81, (f32[2,192]{1,0:T(2,128)S(1)}, s32[512]{0:T(512)S(1)}, s32[192]{0:T(256)S(1)}, ...), branch_computations={%region_7.7_spmd, %region_8.12_spmd} | conditional | flops 103074048 | bytes 3816736 | solution.py:86
  138.5 1.6 %conditional.4 = ((f32[2,192]{1,0:T(2,128)S(1)}, f32[2,192]{1,0:T(2,128)S(1)}, f32[192,256]{1,0:T(8,128)S(1)})) conditional(s32[]{:T(128)} %convert_element_type.59, (f32[2,192]{1,0:T(2,128)S(1)}, f32[2,192]{1,0:T(2,128)S(1)}, f32[192,256]{1,0:T(8,128)S(1)}) %tuple.79, (f32[2,192]{1,0:T(2,128)S(1)}, s32[512]{0:T(512)S(1)}, s32[192]{0:T(256)S(1)}, ...), branch_computations={%region_1.1_spmd, %region_2.6_spmd} | conditional | flops 103074048 | bytes 3816736 | solution.py:86
  141.4 1.1 dynamic-slice_bitcast_fusion.3
  143.7 1.6 %conditional.5 = ((f32[2,192]{1,0:T(2,128)S(1)}, f32[2,192]{1,0:T(2,128)S(1)}, f32[192,256]{1,0:T(8,128)S(1)})) conditional(s32[]{:T(128)} %convert_element_type.60, (f32[2,192]{1,0:T(2,128)S(1)}, f32[2,192]{1,0:T(2,128)S(1)}, f32[192,256]{1,0:T(8,128)S(1)}) %tuple.81, (f32[2,192]{1,0:T(2,128)S(1)}, s32[512]{0:T(512)S(1)}, s32[192]{0:T(256)S(1)}, ...), branch_computations={%region_7.7_spmd, %region_8.12_spmd} | conditional | flops 103074048 | bytes 3816736 | solution.py:86
  (198 shorter events, 32.7 us)
Async XLA Ops:
  7.2 75.8 %all-gather.3.cloned.1.call-start = ((), (), s32[]{:S(2)}) async-start(), calls=%async_computation.2 | async-start | bytes 1769472 | tf_op jit(solution)/shard_map/all_gather | solution.py:99
  7.9 12.4 %copy-start.6 = (s32[3]{0:T(128)S(1)}, s32[3]{0:T(128)}, u32[]{:S(2)}) copy-start(s32[3]{0:T(128)} %param.19) | copy-start | bytes 40
  7.9 12.5 %copy-start.4 = (bf16[384,256]{1,0:T(8,128)(2,1)S(1)}, bf16[384,256]{1,0:T(8,128)(2,1)}, u32[]{:S(2)}) copy-start(bf16[384,256]{1,0:T(8,128)(2,1)} %param.13) | copy-start | bytes 589828
  11.9 29.3 %all-to-all-start = ((bf16[1024,4,256]{0,2,1:T(8,128)(2,1)}), bf16[1024,4,256]{0,2,1:T(8,128)(2,1)S(1)}, u32[]{:S(2)}, u32[]{:S(2)}) async-start(bf16[1024,4,256]{0,2,1:T(8,128)(2,1)} %bitcast.56), calls=%async_computation | async-start | bytes 4194304 | tf_op jit(solution)/shard_map/all_to_all | solution.py:120
  15.5 83.5 %all-gather.5.cloned.1.call-start = ((), (), s32[]{:S(2)}) async-start(), calls=%async_computation.3 | async-start | bytes 1769472 | tf_op jit(solution)/shard_map/all_gather | solution.py:100
  16.3 32.0 %copy-start.5 = (bf16[384,256]{1,0:T(8,128)(2,1)S(1)}, bf16[384,256]{1,0:T(8,128)(2,1)}, u32[]{:S(2)}) copy-start(bf16[384,256]{1,0:T(8,128)(2,1)} %param.16) | copy-start | bytes 589828
  41.2 30.2 %all-to-all-start.1 = ((bf16[1024,4,256]{0,2,1:T(8,128)(2,1)}), bf16[1024,4,256]{0,2,1:T(8,128)(2,1)}, u32[]{:S(2)}, u32[]{:S(2)}) async-start(bf16[1024,4,256]{0,2,1:T(8,128)(2,1)} %bitcast.25), calls=%async_computation.1 | async-start | bytes 4194304 | tf_op jit(solution)/shard_map/all_to_all | solution.py:121
  48.2 2.8 %copy-start.3 = (bf16[4,1024,256]{2,1,0:T(8,128)(2,1)S(1)}, bf16[4,1024,256]{2,1,0:T(8,128)(2,1)}, u32[]{:S(2)}) copy-start(bf16[4,1024,256]{2,1,0:T(8,128)(2,1)} %copy.18) | copy-start | bytes 6291460
  51.0 4.7 %copy-start = (f32[384,4096]{1,0:T(8,128)}, f32[384,4096]{1,0:T(8,128)S(1)}, u32[]{:S(2)}) copy-start(f32[384,4096]{1,0:T(8,128)S(1)} %get-tuple-element.238) | copy-start | bytes 18874372
  52.4 3.3 %copy-start.1 = (f32[384,4096]{1,0:T(8,128)}, f32[384,4096]{1,0:T(8,128)S(1)}, u32[]{:S(2)}) copy-start(f32[384,4096]{1,0:T(8,128)S(1)} %get-tuple-element.240) | copy-start | bytes 18874372
  71.4 8.9 %slice-start = ((s8[6291456]{0:T(1024)(128)(4,1)}), s8[2097152]{0:T(1024)(128)(4,1)S(1)}, s32[]{:S(2)}) async-start(s8[6291456]{0:T(1024)(128)(4,1)} %bitcast.57), calls=%async_computation.4 | async-start | bytes 4194304
  75.5 4.9 %copy-start.2 = (bf16[4,1024,256]{2,1,0:T(8,128)(2,1)S(1)}, bf16[4,1024,256]{2,1,0:T(8,128)(2,1)}, u32[]{:S(2)}) copy-start(bf16[4,1024,256]{2,1,0:T(8,128)(2,1)} %copy.20) | copy-start | bytes 6291460
  75.5 4.9 %slice-start.1 = ((s8[6291456]{0:T(1024)(128)(4,1)}), s8[4194304]{0:T(1024)(128)(4,1)S(1)}, s32[]{:S(2)}) async-start(s8[6291456]{0:T(1024)(128)(4,1)} %bitcast.57), calls=%async_computation.5 | async-start | bytes 8388608
Sparse Core Ops, SparseCore 0:
  10.2 43.9 all-gather.2
  56.4 42.6 all-gather.4
where the time goes:
time: 156 us; the launch traced here: 155 us
  waiting for transfers between devices  53.9 us (35%)
  local copies, waits for them, and re-layouts  34.4 us (22%)
  matrix products  23.4 us (15%)
  between operations  14.3 us (9%)
  loops' own time  12.5 us (8%)
  other arithmetic  8.48 us (5%)
  starting transfers between devices  8.15 us (5%)
    all_to_all x1, waiting for transfers between devices, per_device(): lax.all_to_all(text_k, 'txt', split_axis=1, concat_axis=0, tiled=True)  20.8 us
    all_gather x1, waiting for transfers between devices, per_device(): values = lax.all_gather(self_v, 'seq', axis=0, tiled=True)  16.1 us
    all_to_all x1, waiting for transfers between devices, per_device(): lax.all_to_all(text_v, 'txt', split_axis=1, concat_axis=0, tiled=True)  15.7 us
    dot_general x24, matrix products, softmax_update(): jnp.dot(probs.astype(jnp.bfloat16), values[:, low:high], preferred_elemen...  12.4 us
    another operation x1, loops' own time, per_device(): lax.scan(one_block, carry, (key_blocks, value_blocks, jnp.arange(length /...  11.7 us
    dot_general x24, matrix products, softmax_update(): lax.dot_general(query[:, low:high], keys[:, low:high], (((1,), (1,)), (()...  11 us
    unnamed x21, local copies, waits for them, and re-layouts  8.92 us
    slice x12, local copies, waits for them, and re-layouts, visit(): positions[group][half - 1]  7.75 us
  transfers between devices with their start and end apart: 4, of which 3 were waited for; matrix products, arithmetic and copies ran while one was open for 19% of the time, Pallas kernels for 0%

commit v1 on v0

v1 whole, which is shorter than its diff:
```python
import functools
import math

import jax
import jax.numpy as jnp
from jax import lax
from jax.experimental import pallas as pl
from jax.experimental.pallas import tpu as pltpu
from jax.sharding import PartitionSpec as P

HSIZE = 128
SPAN = 128
TBLK = 128

NEG = -1e30
FLOOR = -1e20
SCALE = math.log2(math.e) / math.sqrt(HSIZE)
MESH = pl.DeviceIdType.MESH


def scores_of(query, keys):
    return (
        lax.dot_general(
            query, keys, (((1,), (1,)), ((), ())), preferred_element_type=jnp.float32
        )
        * SCALE
    )


def pack_stats(columns):
    rows = columns[0].shape[0]
    lane = lax.broadcasted_iota(jnp.int32, (rows, HSIZE), 1)
    tile = jnp.zeros((rows, HSIZE), jnp.float32)
    for at, column in enumerate(columns):
        tile = jnp.where(lane == at, column, tile)
    return jnp.transpose(tile)[:8]


def unpack_stats(packed, count):
    full = jnp.concatenate(
        [packed, jnp.zeros((HSIZE - 8, packed.shape[1]), jnp.float32)], axis=0
    )
    tile = jnp.transpose(full)
    return [tile[:, at : at + 1] for at in range(count)]


def kernel(
    S, T, rows, H, text,
    lags, q, k, v, cq, tk, tv,
    self_out, cross_out,
    qp, kbuf, vbuf, acc, top, tot,
    pair_out, pair_in, pstat_out, pstat_in,
    cqb, tkb, tvb, cown, ctop, ctot,
    part_out, part_in, cstat_out, cstat_in,
    loc_sem, txt_sem, q_send, q_recv, kv_send, kv_recv,
    cq_send, cq_recv, pair_send, pair_recv, part_send, part_recv,
):
    me = lax.axis_index("seq")
    t = lax.axis_index("txt")
    nz = S // 2
    z = me // 2
    y = me % 2
    partner = me + 1 - 2 * y
    up = (me + 2) % S
    width = H * HSIZE

    if T == 4:
        peers = [t, t + 1 - 2 * (t % 2), t + 2 - 4 * (t // 2), 3 - t]
        owners = peers
    else:
        peers = [(t + r) % T for r in range(T)]
        owners = [(t + T - r) % T for r in range(T)]

    def cols(h):
        return pl.ds(h * HSIZE, HSIZE)

    locals_ = []

    def local(src, dst, sem):
        copy = pltpu.make_async_copy(src, dst, sem)
        copy.start()
        return copy

    own_cq = local(cq, cqb.at[0], loc_sem.at[0])
    text_copies = []
    for r in range(T):
        at = pl.ds(pl.multiple_of(owners[r] * width, HSIZE), width)
        text_copies.append(
            (
                local(tk.at[:, at], tkb.at[r], txt_sem.at[r, 0]),
                local(tv.at[:, at], tvb.at[r], txt_sem.at[r, 1]),
            )
        )
    for h in range(H):
        locals_.append(local(q.at[:, cols(h)], qp.at[h, pl.ds(0, rows)], loc_sem.at[1 + 3 * h]))
        locals_.append(local(k.at[:, cols(h)], kbuf.at[0, h], loc_sem.at[2 + 3 * h]))
        locals_.append(local(v.at[:, cols(h)], vbuf.at[0, h], loc_sem.at[3 + 3 * h]))

    barrier = pltpu.get_barrier_semaphore()
    pl.semaphore_signal(barrier, inc=1, device_id=(partner, t), device_id_type=MESH)
    for r in range(1, T):
        pl.semaphore_signal(barrier, inc=1, device_id=(me, peers[r]), device_id_type=MESH)

    @pl.when(z < nz - 1)
    def _():
        pl.semaphore_signal(barrier, inc=1, device_id=(me + 2, t), device_id_type=MESH)

    @pl.when(z > 0)
    def _():
        pl.semaphore_signal(barrier, inc=1, device_id=(me - 2, t), device_id_type=MESH)

    pl.semaphore_wait(barrier, T + jnp.minimum(z, 1) + jnp.minimum(nz - 1 - z, 1))

    def remote(src, dst, send, recv, device):
        return pltpu.make_async_remote_copy(
            src_ref=src, dst_ref=dst, send_sem=send, recv_sem=recv,
            device_id=device, device_id_type=MESH,
        )

    def kv_copy(d, h, which, src=None):
        buf = (kbuf, vbuf)[which]
        return remote(
            buf.at[d, h] if src is None else src, buf.at[d + 1, h],
            kv_send.at[d, h, which], kv_recv.at[d + 1, h, which], (up, t),
        )

    def own_kv(h, which):
        return kv_copy(0, h, which, (k, v)[which].at[:, cols(h)])

    @pl.when(z < nz - 1)
    def _():
        for h in range(H):
            own_kv(h, 0).start()
            own_kv(h, 1).start()

    q_copies = [
        remote(q.at[:, cols(h)], qp.at[h, pl.ds(rows, rows)], q_send.at[h], q_recv.at[h], (partner, t))
        for h in range(H)
    ]
    cq_copies = [None] + [
        remote(cq, cqb.at[r], cq_send.at[r], cq_recv.at[r], (me, peers[r])) for r in range(1, T)
    ]
    for r in range(1, T):
        cq_copies[r].start()
    for copy in q_copies:
        copy.start()

    row_id = lax.broadcasted_iota(jnp.int32, (rows, 1), 0)
    limit = jnp.full((rows, 1), lags[0] * TBLK, jnp.int32)
    for c in range(1, rows // SPAN):
        limit = jnp.where(row_id >= c * SPAN, lags[c] * TBLK, limit)
    limit = limit - t * text

    def cross_head(r, h):
        low = h * HSIZE
        s = scores_of(cqb[r, :, low : low + HSIZE], tkb[r, :, low : low + HSIZE])
        col = lax.broadcasted_iota(jnp.int32, (rows, text), 1)
        s = jnp.where(col < limit, s, NEG)
        peak = jnp.maximum(jnp.max(s, axis=1, keepdims=True), FLOOR)
        p = jnp.exp2(s - peak)
        total = jnp.sum(p, axis=1, keepdims=True)
        mixed = jnp.dot(
            p.astype(jnp.bfloat16), tvb[r, :, low : low + HSIZE], preferred_element_type=jnp.float32
        )
        return peak, total, mixed

    part_copies = {}

    def cross(r):
        for copy in text_copies[r]:
            copy.wait()
        if r == 0:
            own_cq.wait()
        else:
            cq_copies[r].wait_recv()
        stats = []
        for h in range(H):
            low = h * HSIZE
            peak, total, mixed = cross_head(r, h)
            if r == 0:
                cown[:, low : low + HSIZE] = mixed
                ctop[h] = peak
                ctot[h] = total
            else:
                part_out[r, :, low : low + HSIZE] = mixed.astype(jnp.bfloat16)
                stats += [peak, total]
        if r > 0:
            cstat_out[r] = pack_stats(stats)
            pair = (
                remote(part_out.at[r], part_in.at[r], part_send.at[r, 0], part_recv.at[r, 0], (me, owners[r])),
                remote(cstat_out.at[r], cstat_in.at[r], part_send.at[r, 1], part_recv.at[r, 1], (me, owners[r])),
            )
            for copy in pair:
                copy.start()
            part_copies[r] = pair

    def first_half(h, half):
        part = pl.ds(half * rows, rows)
        s = scores_of(qp[h, part], kbuf[0, h])
        if half == 0:
            i = lax.broadcasted_iota(jnp.int32, (rows, rows), 0)
            j = lax.broadcasted_iota(jnp.int32, (rows, rows), 1)
            s = jnp.where(j <= i, s, NEG)
        else:
            s = s + y.astype(jnp.float32) * NEG
        peak = jnp.maximum(jnp.max(s, axis=1, keepdims=True), FLOOR)
        p = jnp.exp2(s - peak)
        top[h, part] = peak
        tot[h, part] = jnp.sum(p, axis=1, keepdims=True)
        acc[h, part] = jnp.dot(
            p.astype(jnp.bfloat16), vbuf[0, h], preferred_element_type=jnp.float32
        )

    def item(n, carry):
        d = n // H + 1
        h = n % H
        kv_copy(d - 1, h, 0).wait_recv()
        kv_copy(d - 1, h, 1).wait_recv()

        @pl.when(z < nz - 1)
        def _():
            kv_copy(d, h, 0).start()
            kv_copy(d, h, 1).start()

        for half in range(2):
            part = pl.ds(half * rows, rows)
            s = scores_of(qp[h, part], kbuf[d, h])
            before = top[h, part]
            peak = jnp.maximum(before, jnp.max(s, axis=1, keepdims=True))
            p = jnp.exp2(s - peak)
            shrink = jnp.exp2(before - peak)
            top[h, part] = peak
            tot[h, part] = tot[h, part] * shrink + jnp.sum(p, axis=1, keepdims=True)
            acc[h, part] = acc[h, part] * shrink + jnp.dot(
                p.astype(jnp.bfloat16), vbuf[d, h], preferred_element_type=jnp.float32
            )
        return carry

    items = H * z
    cross(0)
    if T > 1:
        cross(1)
    for copy in locals_:
        copy.wait()
    for h in range(H):
        first_half(h, 0)
    for copy in q_copies:
        copy.wait_recv()
    for h in range(H):
        first_half(h, 1)
    done = 0
    for r in range(2, T):
        lax.fori_loop(jnp.minimum(done, items), jnp.minimum(done + 2, items), item, 0)
        done += 2
        cross(r)
    lax.fori_loop(jnp.minimum(done, items), items, item, 0)

    theirs = pl.ds(rows, rows)
    mine = pl.ds(0, rows)
    pair_copies = []
    for h in range(H):
        pair_out[h] = acc[h, theirs].astype(jnp.bfloat16)
        pstat_out[h] = pack_stats([top[h, theirs], tot[h, theirs]])
        for copy in (
            remote(pair_out.at[h], pair_in.at[h], pair_send.at[h, 0], pair_recv.at[h, 0], (partner, t)),
            remote(pstat_out.at[h], pstat_in.at[h], pair_send.at[h, 1], pair_recv.at[h, 1], (partner, t)),
        ):
            copy.start()
            pair_copies.append(copy)

    arrived = []
    for r in range(1, T):
        for copy in part_copies[r]:
            copy.wait_recv()
        arrived.append(unpack_stats(cstat_in[r], 2 * H))
    for h in range(H):
        low = h * HSIZE
        peak = ctop[h]
        for stats in arrived:
            peak = jnp.maximum(peak, stats[2 * h])
        weight = jnp.exp2(ctop[h] - peak)
        total = ctot[h] * weight
        mixed = cown[:, low : low + HSIZE] * weight
        for r in range(1, T):
            weight = jnp.exp2(arrived[r - 1][2 * h] - peak)
            total = total + arrived[r - 1][2 * h + 1] * weight
            mixed = mixed + part_in[r, :, low : low + HSIZE].astype(jnp.float32) * weight
        cross_out[:, low : low + HSIZE] = (mixed / total).astype(jnp.bfloat16)

    for h in range(H):
        low = h * HSIZE
        pair_copies[2 * h].wait_recv()
        pair_copies[2 * h + 1].wait_recv()
        other_top, other_tot = unpack_stats(pstat_in[h], 2)
        peak = jnp.maximum(top[h, mine], other_top)
        a = jnp.exp2(top[h, mine] - peak)
        b = jnp.exp2(other_top - peak)
        total = tot[h, mine] * a + other_tot * b
        mixed = acc[h, mine] * a + pair_in[h].astype(jnp.float32) * b
        self_out[:, low : low + HSIZE] = (mixed / total).astype(jnp.bfloat16)

    for copy in pair_copies + q_copies + cq_copies[1:]:
        copy.wait_send()
    for r in range(1, T):
        for copy in part_copies[r]:
            copy.wait_send()

    @pl.when(z < nz - 1)
    def _():
        for h in range(H):
            own_kv(h, 0).wait_send()
            own_kv(h, 1).wait_send()

        def drain(n, carry):
            kv_copy(n // H + 1, n % H, 0).wait_send()
            kv_copy(n // H + 1, n % H, 1).wait_send()
            return carry

        lax.fori_loop(0, items, drain, 0)


def per_device(S, T, self_q, self_k, self_v, cross_q, text_k, text_v, lags):
    rows, width = self_q.shape
    text = text_k.shape[0]
    H = width // HSIZE
    nz = S // 2
    bf16, f32 = jnp.bfloat16, jnp.float32
    vmem = pltpu.VMEM
    dma = pltpu.SemaphoreType.DMA
    any_spec = pl.BlockSpec(memory_space=pl.ANY)
    return pl.pallas_call(
        functools.partial(kernel, S, T, rows, H, text),
        out_shape=(jax.ShapeDtypeStruct((rows, width), bf16),) * 2,
        in_specs=[pl.BlockSpec(memory_space=pltpu.SMEM)] + [any_spec] * 6,
        out_specs=(pl.BlockSpec(memory_space=vmem),) * 2,
        scratch_shapes=[
            vmem((H, 2 * rows, HSIZE), bf16),
            vmem((nz, H, rows, HSIZE), bf16),
            vmem((nz, H, rows, HSIZE), bf16),
            vmem((H, 2 * rows, HSIZE), f32),
            vmem((H, 2 * rows, 1), f32),
            vmem((H, 2 * rows, 1), f32),
            vmem((H, rows, HSIZE), bf16),
            vmem((H, rows, HSIZE), bf16),
            vmem((H, 8, rows), f32),
            vmem((H, 8, rows), f32),
            vmem((T, rows, width), bf16),
            vmem((T, text, width), bf16),
            vmem((T, text, width), bf16),
            vmem((rows, width), f32),
            vmem((H, rows, 1), f32),
            vmem((H, rows, 1), f32),
            vmem((T, rows, width), bf16),
            vmem((T, rows, width), bf16),
            vmem((T, 8, rows), f32),
            vmem((T, 8, rows), f32),
            dma((1 + 3 * H,)),
            dma((T, 2)),
            dma((H,)),
            dma((H,)),
            dma((nz, H, 2)),
            dma((nz + 1, H, 2)),
            dma((T,)),
            dma((T,)),
            dma((H, 2)),
            dma((H, 2)),
            dma((T, 2)),
            dma((T, 2)),
        ],
        compiler_params=pltpu.CompilerParams(
            collective_id=0, has_side_effects=True, vmem_limit_bytes=48 * 1024 * 1024
        ),
        cost_estimate=pl.CostEstimate(
            flops=4 * rows * width * (T * text + nz * 2 * rows),
            bytes_accessed=4 * text * T * width,
            transcendentals=rows * H * (T * text + nz * 2 * rows),
        ),
    )(lags, self_q, self_k, self_v, cross_q, text_k, text_v)


def solution(mesh):
    S, T = mesh.shape["seq"], mesh.shape["txt"]
    return jax.shard_map(
        functools.partial(per_device, S, T),
        mesh=mesh,
        in_specs=(
            P("seq", "txt"),
            P("seq", "txt"),
            P("seq", "txt"),
            P("seq", "txt"),
            P("txt", None),
            P("txt", None),
            P("seq"),
        ),
        out_specs=(P("seq", "txt"), P("seq", "txt")),
        check_vma=False,
    )
```

time: 156 us -> 49.5 us (0.32)
  waiting for transfers between devices: 53.9 us -> 0 us
  Pallas kernels: 0 us -> 39.7 us
  local copies, waits for them, and re-layouts: 34.4 us -> 8.89 us
  matrix products: 23.4 us -> 0 us
  between operations: 14.3 us -> 0.66 us
  loops' own time: 12.5 us -> 0 us
  other arithmetic: 8.48 us -> 0 us
  starting transfers between devices: 8.15 us -> 0 us
    pallas_call x0 -> x1, Pallas kernels: none -> 39.7 us  [per_device(): pl.pallas_call(functools.partial(kernel, S, T, rows, H, text), out_shape=...]
    all_to_all x2 -> x0, waiting for transfers between devices: 36.4 us -> none  [the longest x1 20.8 us: per_device(): lax.all_to_all(text_k, 'txt', split_axis=1, concat_axis=0, tiled=True)]
    dot_general x48 -> x0, matrix products: 23.4 us -> none  [the longest x24 12.4 us: softmax_update(): jnp.dot(probs.astype(jnp.bfloat16), values[:, low:high], preferred_elemen...]
    all_gather x2 -> x0, waiting for transfers between devices: 16.1 us -> none  [the longest x1 16.1 us: per_device(): values = lax.all_gather(self_v, 'seq', axis=0, tiled=True)]
    another operation x13 -> x0, loops' own time: 12.5 us -> none  [the longest x1 11.7 us: per_device(): lax.scan(one_block, carry, (key_blocks, value_blocks, jnp.arange(length /...]
    all_to_all x2 -> x0, starting transfers between devices: 8.07 us -> none  [the longest x1 4.47 us: per_device(): lax.all_to_all(text_v, 'txt', split_axis=1, concat_axis=0, tiled=True)]
    slice x24 -> x0, local copies, waits for them, and re-layouts: 7.82 us -> none  [the longest x12 7.75 us: visit(): positions[group][half - 1]]
    reduce_sum x12 -> x0, other arithmetic: 6.99 us -> none  [softmax_update(): sums.append(totals[head] * shrink + jnp.sum(probs, axis=1))]
  transfers between devices with their start and end apart: 4 -> 0, of which waited for: 3 -> 0; matrix products, arithmetic and copies ran while one was open for 19% -> 0% of each run, Pallas kernels for 0% -> 0%
where the time goes in v1:
time: 49.5 us; the launch traced here: 49.2 us
  Pallas kernels  39.7 us (80%)
  local copies, waits for them, and re-layouts  8.89 us (18%)
  between operations  0.66 us (1%)
    pallas_call x1, Pallas kernels, per_device(): pl.pallas_call(functools.partial(kernel, S, T, rows, H, text), out_shape=...  39.7 us
    unnamed x16, local copies, waits for them, and re-layouts  8.89 us

profile of v1, /device:TPU:24, one launch (start us, length us, event | category | flops | bytes accessed | tf_op | source)
XLA Modules:
  0.0 49.2 jit_solution(17643435305267782413)
XLA Ops:
  0.6 0.0 copy-start
  0.6 1.6 %copy-done = bf16[1024,1024]{1,0:T(8,128)(2,1)S(1)} copy-done((bf16[1024,1024]{1,0:T(8,128)(2,1)S(1)}, bf16[1024,1024]{1,0:T(8,128)(2,1)}, u32[]{:S(2)}) %copy-start) | copy-done | bytes 2097176
  2.2 0.0 copy-start.1
  2.2 1.6 %copy-done.1 = bf16[1024,1024]{1,0:T(8,128)(2,1)S(1)} copy-done((bf16[1024,1024]{1,0:T(8,128)(2,1)S(1)}, bf16[1024,1024]{1,0:T(8,128)(2,1)}, u32[]{:S(2)}) %copy-start.1) | copy-done | bytes 2097176
  3.8 0.0 copy-start.2
  3.8 0.9 %copy-done.2 = bf16[384,256]{1,0:T(8,128)(2,1)S(1)} copy-done((bf16[384,256]{1,0:T(8,128)(2,1)S(1)}, bf16[384,256]{1,0:T(8,128)(2,1)}, u32[]{:S(2)}) %copy-start.2) | copy-done | bytes 196632
  4.7 0.0 copy-start.3
  4.7 0.9 %copy-done.3 = bf16[384,256]{1,0:T(8,128)(2,1)S(1)} copy-done((bf16[384,256]{1,0:T(8,128)(2,1)S(1)}, bf16[384,256]{1,0:T(8,128)(2,1)}, u32[]{:S(2)}) %copy-start.3) | copy-done | bytes 196632
  5.7 0.0 copy-start.4
  5.7 0.9 %copy-done.4 = bf16[384,256]{1,0:T(8,128)(2,1)S(1)} copy-done((bf16[384,256]{1,0:T(8,128)(2,1)S(1)}, bf16[384,256]{1,0:T(8,128)(2,1)}, u32[]{:S(2)}) %copy-start.4) | copy-done | bytes 196632
  6.6 0.0 copy-start.5
  6.6 0.9 %copy-done.5 = bf16[384,256]{1,0:T(8,128)(2,1)S(1)} copy-done((bf16[384,256]{1,0:T(8,128)(2,1)S(1)}, bf16[384,256]{1,0:T(8,128)(2,1)}, u32[]{:S(2)}) %copy-start.5) | copy-done | bytes 196632
  7.5 0.0 copy-start.6
  7.5 0.7 %copy-done.6 = s32[3]{0:T(128)S(1)} copy-done((s32[3]{0:T(128)S(1)}, s32[3]{0:T(128)}, u32[]{:S(2)}) %copy-start.6) | copy-done | bytes 36
  8.2 39.7 %shard_map.86 = (bf16[384,256]{1,0:T(8,128)(2,1)S(1)}, bf16[384,256]{1,0:T(8,128)(2,1)S(1)}) custom-call(s32[3]{0:T(128)S(1)} %copy-done.6, bf16[384,256]{1,0:T(8,128)(2,1)S(1)} %copy-done.2, bf16[384,256]{1,0:T(8,128)(2,1)S(1)} %copy-done.3, bf16[384,256]{1,0:T(8,128)(2,1)S(1)} %copy-done.4, bf16[384,256]{1,0:T(8,128)(2,1)S(1)} %copy-done.5, ...), custom_call_target="tpu_custom_call" | custom-call | flops 2818572288 | bytes 4194304 | tf_op jit(solution)/shard_map/pallas_call | solution.py:331
  47.8 0.7 %copy.11 = bf16[384,256]{1,0:T(8,128)(2,1)} copy(bf16[384,256]{1,0:T(8,128)(2,1)S(1)} %get-tuple-element.4) | data formatting | bytes 393216
  48.5 0.7 %copy.12 = bf16[384,256]{1,0:T(8,128)(2,1)} copy(bf16[384,256]{1,0:T(8,128)(2,1)S(1)} %get-tuple-element.5) | data formatting | bytes 393216
Async XLA Ops:
  0.6 1.6 %copy-start = (bf16[1024,1024]{1,0:T(8,128)(2,1)S(1)}, bf16[1024,1024]{1,0:T(8,128)(2,1)}, u32[]{:S(2)}) copy-start(bf16[1024,1024]{1,0:T(8,128)(2,1)} %tk.1) | copy-start | bytes 6291460
  2.2 1.6 %copy-start.1 = (bf16[1024,1024]{1,0:T(8,128)(2,1)S(1)}, bf16[1024,1024]{1,0:T(8,128)(2,1)}, u32[]{:S(2)}) copy-start(bf16[1024,1024]{1,0:T(8,128)(2,1)} %tv.1) | copy-start | bytes 6291460
  3.8 0.9 %copy-start.2 = (bf16[384,256]{1,0:T(8,128)(2,1)S(1)}, bf16[384,256]{1,0:T(8,128)(2,1)}, u32[]{:S(2)}) copy-start(bf16[384,256]{1,0:T(8,128)(2,1)} %q.1) | copy-start | bytes 589828
  4.7 0.9 %copy-start.3 = (bf16[384,256]{1,0:T(8,128)(2,1)S(1)}, bf16[384,256]{1,0:T(8,128)(2,1)}, u32[]{:S(2)}) copy-start(bf16[384,256]{1,0:T(8,128)(2,1)} %k.1) | copy-start | bytes 589828
  5.7 0.9 %copy-start.4 = (bf16[384,256]{1,0:T(8,128)(2,1)S(1)}, bf16[384,256]{1,0:T(8,128)(2,1)}, u32[]{:S(2)}) copy-start(bf16[384,256]{1,0:T(8,128)(2,1)} %v.1) | copy-start | bytes 589828
  6.6 0.9 %copy-start.5 = (bf16[384,256]{1,0:T(8,128)(2,1)S(1)}, bf16[384,256]{1,0:T(8,128)(2,1)}, u32[]{:S(2)}) copy-start(bf16[384,256]{1,0:T(8,128)(2,1)} %cq.1) | copy-start | bytes 589828
  7.5 0.7 %copy-start.6 = (s32[3]{0:T(128)S(1)}, s32[3]{0:T(128)}, u32[]{:S(2)}) copy-start(s32[3]{0:T(128)} %lags.1) | copy-start | bytes 40
